TPU v7x, 32 devices: a whole 2x2x4 slice. The times are simulated.
32 devices in a mesh: leaf: 2 (over x), grid: 16 (over z, y, core).
Axes of the slice: x: 2, y: 2, z: 4, core: 2. Of those that a mesh axis runs over, the one named last changes fastest.
Arguments:
- front_diag: float32 [2, 8192], P('leaf', 'grid'), may hold values from 1 to 4
- children: bfloat16 [4, 4096, 4096], P('leaf', 'grid'), may hold values from 0 to 1, as said below
- parent: int32 [4], replicated, may hold values from 0 to 1, as said below
- front_blocks: int32 [2], replicated, may hold values from 64 to 128
- child_blocks: int32 [4], replicated, may hold values from 32 to 64
- row_map: int32 [4, 64], replicated, may hold values from 0 to 127, as said below
Outputs:
- factor: bfloat16 [2, 8192, 8192], P('leaf', 'grid')
Inputs may be any that keep to these rules, and one draw needn't show every extreme that they name: Children 2 l and 2 l + 1 belong to leaf index l; one of them has parent l and the other has parent l xor 1, so each front has exactly two children. Each row_map[c] holds 64 distinct increasing block numbers, all below front_blocks[parent[c]]; only its first child_blocks[c] entries are used. Each children[c] is symmetric.
All inputs are finite; a program needn't handle non-finite values.
Results may differ from a plain program's by a relative error of at most 0.003.
The roundings to bfloat16 on the way count: a program that leaves them out, or rounds other values in their place, can miss the bound.
Values may be sent and summed in bfloat16 or wider, within the bound.
A program may use at most 128 MiB of HBM per device.

v0:
```python
import jax
import jax.numpy as jnp
from jax import lax
from jax.sharding import PartitionSpec as P

BLK = 64
PW = 256
PANELS = 3


def swapped(value, axis, distance):
    mask = 2**distance
    pairs = [(source, source ^ mask) for source in range(lax.axis_size(axis))]
    return lax.ppermute(value, axis, pairs)


def pivot_parts(pivot_block):
    pivot_factor = jnp.linalg.cholesky(pivot_block)
    identity = jnp.eye(PW, dtype=jnp.float32)
    pivot_inverse = jax.scipy.linalg.solve_triangular(pivot_factor, identity, lower=True)
    return (pivot_factor, pivot_inverse)


def pivot_rows(panel_cols, row_ids, left_edge):
    selector = (jnp.arange(PW)[:, None] + left_edge == row_ids[None, :]).astype(jnp.float32)
    return jnp.dot(selector, panel_cols.astype(jnp.float32), precision=lax.Precision.HIGHEST)


def panel_factor(panel_cols, row_ids, left_edge, pivot_factor, pivot_inverse):
    right_edge = left_edge + PW
    solved = jnp.dot(
        panel_cols.astype(jnp.float32), pivot_inverse.T, precision=lax.Precision.HIGHEST
    )
    selector = (row_ids[:, None] - left_edge == jnp.arange(PW)[None, :]).astype(jnp.float32)
    diagonal_rows = jnp.dot(selector, pivot_factor, precision=lax.Precision.HIGHEST)
    picked = jnp.where(row_ids[:, None] < right_edge, diagonal_rows, solved)
    return jnp.where(row_ids[:, None] < left_edge, jnp.float32(0.0), picked).astype(jnp.bfloat16)


def renew(previous, own_factor, portion, row_ids, right_edge):
    length = portion.shape[0]
    product = lax.dot_general(
        own_factor, portion, (((1,), (1,)), ((), ())), preferred_element_type=jnp.float32
    )
    col_ids = jnp.arange(length)
    renewed = (previous.astype(jnp.float32) - product).astype(jnp.bfloat16)
    tail_cols = col_ids[None, :] >= right_edge
    tail_rows = row_ids[:, None] >= right_edge
    return jnp.where(tail_cols, jnp.where(tail_rows, renewed, jnp.zeros_like(renewed)), previous)


def body(front_diag, children, parent, front_blocks, child_blocks, row_map):
    leaf_id = lax.axis_index("leaf")
    grid_id = lax.axis_index("grid")
    rows_here = front_diag.shape[1]
    front_order = rows_here * lax.axis_size("grid")
    child_rows = children.shape[1]
    child_order = children.shape[2]
    blocks_front = front_order // BLK
    blocks_child = child_order // BLK
    partner = jnp.bitwise_xor(leaf_id, 1)
    first_child = 2 * leaf_id
    keep_first = parent[first_child] == leaf_id
    own_part = jnp.where(keep_first, children[0], children[1])
    away_part = jnp.where(keep_first, children[1], children[0])
    own_child = jnp.where(keep_first, first_child, first_child + 1)
    partner_first = 2 * partner
    far_child = jnp.where(parent[partner_first] == leaf_id, partner_first, partner_first + 1)
    arrived = swapped(away_part, "leaf", 0)
    stacked = jnp.stack([own_part, arrived])
    child_ids = jnp.stack([own_child, far_child])
    block_maps = row_map[child_ids]
    counts = child_blocks[child_ids]
    target_blocks = jnp.arange(blocks_front)[None, None, :]
    live_blocks = jnp.arange(blocks_child)[None, :, None] < counts[:, None, None]
    onehot = ((block_maps[:, :, None] == target_blocks) & live_blocks).astype(jnp.bfloat16)
    spread = jnp.einsum(
        "srbk,sbq->srqk",
        stacked.reshape(2, child_rows, blocks_child, BLK),
        onehot,
        preferred_element_type=jnp.bfloat16,
    ).reshape(2, child_rows, front_order)
    received = lax.all_to_all(spread, "grid", split_axis=2, concat_axis=1, tiled=True)
    placed = jnp.einsum(
        "sbkj,sbq->sjqk",
        received.reshape(2, blocks_child, BLK, rows_here),
        onehot,
        preferred_element_type=jnp.bfloat16,
    ).reshape(2, rows_here, front_order)
    row_ids = grid_id * rows_here + jnp.arange(rows_here)
    col_ids = jnp.arange(front_order)
    active = front_blocks[leaf_id] * BLK
    on_diag = row_ids[:, None] == col_ids[None, :]
    summed = placed[0].astype(jnp.float32) + placed[1].astype(jnp.float32)
    summed = summed + jnp.where(on_diag, front_diag[0][:, None], jnp.float32(0.0))
    padding = (row_ids[:, None] >= active) | (col_ids[None, :] >= active)
    identity_part = jnp.where(on_diag, jnp.float32(1.0), jnp.float32(0.0))
    matrix = jnp.where(padding, identity_part, summed).astype(jnp.bfloat16)
    for step in range(PANELS):
        left_edge = step * PW
        right_edge = left_edge + PW
        pivot_block = lax.psum(
            pivot_rows(matrix[:, left_edge:right_edge], row_ids, left_edge), "grid"
        )
        pivot_factor, pivot_inverse = pivot_parts(pivot_block)
        own_factor = panel_factor(
            matrix[:, left_edge:right_edge], row_ids, left_edge, pivot_factor, pivot_inverse
        )

        def trailing(portion, offset, current=matrix, own_rows=own_factor, edge=right_edge):
            return renew(current, own_rows, portion, row_ids, edge)

        matrix = trailing(lax.all_gather(own_factor, "grid", axis=0, tiled=True), jnp.int32(0))
        matrix = matrix.at[:, left_edge:right_edge].set(own_factor)
    return matrix[None]


def solution(mesh):
    in_specs = (P("leaf", "grid"), P("leaf", "grid", None), P(), P(), P(), P())
    out_specs = P("leaf", "grid", None)
    return jax.shard_map(body, mesh=mesh, in_specs=in_specs, out_specs=out_specs, check_vma=False)
```

profile of v0, /device:TPU:0, one launch (start us, length us, event | category | flops | bytes accessed | tf_op | source)
XLA Modules:
  0.0 1086.6 jit_solution(10575802746965637004)
XLA Ops:
  6.5 1.3 fusion.121
  8.5 3.9 fusion.120
  12.4 4.1 copy.64
  16.6 2.4 copy.65
  19.0 3.8 broadcast_select_fusion
  22.8 2.9 collective-permute-start
  27.7 1.2 copy.45
  28.9 42.8 %collective-permute-done = bf16[256,4096]{0,1:T(8,128)(2,1)} collective-permute-done((bf16[256,4096]{0,1:T(8,128)(2,1)}, bf16[256,4096]{0,1:T(8,128)(2,1)}, u32[]{:S(2)}, u32[]{:S(2)}) %collective-permute-start) | collective-permute-done | bytes 2097184 | tf_op jit(solution)/shard_map/ppermute | solution.py:14
  71.7 2.8 copy.46
  74.5 4.8 convolution_bitcast_fusion.1
  79.2 11.4 %copy.47 = bf16[2,256,128,64]{1,3,2,0:T(8,128)(2,1)} copy(bf16[2,256,128,64]{1,2,3,0:T(8,128)(2,1)} %convolution_bitcast_fusion.1) | data formatting | bytes 16777216 | tf_op jit(solution)/shard_map/srbk,sbq->srqk/transpose | solution.py:77
  90.6 16.4 %copy.48 = bf16[2,256,8192]{1,0,2:T(2,128)(2,1)} copy(bf16[2,256,8192]{1,2,0:T(8,128)(2,1)} %bitcast.134) | data formatting | bytes 16777216 | tf_op jit(solution)/shard_map/reshape | solution.py:82
  107.0 6.4 all-to-all-start
  114.9 149.2 %all-to-all-done = bf16[2,256,8192]{1,0,2:T(2,128)(2,1)} async-done(((bf16[2,256,8192]{1,0,2:T(2,128)(2,1)}), bf16[2,256,8192]{1,0,2:T(2,128)(2,1)}, u32[]{:S(2)}, u32[]{:S(2)}) %all-to-all-start) | async-done | bytes 8388640 | tf_op jit(solution)/shard_map/all_to_all | solution.py:83
  264.1 7.9 copy.49
  272.0 11.9 %copy.50 = bf16[2,16,256,512]{3,2,1,0:T(8,128)(2,1)} copy(bf16[2,16,256,512]{2,3,1,0:T(8,128)(2,1)} %bitcast.135) | data formatting | bytes 16777216 | tf_op jit(solution)/shard_map/all_to_all | solution.py:83
  283.8 19.6 %convolution_bitcast_fusion = bf16[2,512,128,64]{1,2,3,0:T(8,128)(2,1)} fusion(bf16[2,64,64,512]{3,2,1,0:T(8,128)(2,1)} %bitcast.133, s32[2,64]{1,0:T(2,128)S(1)} %gather_fusion, pred[2,64]{1,0:T(4,128)(4,1)S(1)} %iota_compare_fusion.18), kind=kOutput, calls=%fused_computation.14 | convolution fusion | flops 1073774592 | bytes 25166464 | tf_op jit(solution)/shard_map/sbkj,sbq->sjqk/dot_general | solution.py:84
  303.4 7.3 convert_add_fusion
  310.8 19.6 %copy.52 = f32[1,512,128,64]{1,3,2,0:T(8,128)} copy(f32[1,512,128,64]{1,2,3,0:T(8,128)S(1)} %convert_add_fusion) | data formatting | bytes 33554432 | tf_op jit(solution)/shard_map/add | solution.py:94
  330.4 26.3 %copy.53 = f32[512,8192]{1,0:T(8,128)} copy(f32[512,8192]{0,1:T(8,128)} %bitcast.132) | data formatting | bytes 33554432 | tf_op jit(solution)/shard_map/add | solution.py:94
  356.7 9.7 select_convert_fusion
  366.5 3.4 copy-done.3
  371.0 120.7 %all-reduce.5.cloned.1.call-done = f32[256,256]{0,1:T(8,128)} async-done(((f32[256,256]{0,1:T(8,128)}), f32[256,256]{0,1:T(8,128)}) %all-reduce.5.cloned.1.call-update) | async-done | bytes 262160 | tf_op jit(solution)/shard_map/psum | solution.py:102
  493.8 11.7 %cholesky.172 = f32[128,128]{1,0:T(8,128)S(1)} custom-call(f32[128,128]{1,0:T(8,128)S(1)} %cholesky.270), custom_call_target="Cholesky" | custom-call | tf_op jit(solution)/shard_map/jit(cholesky)/cholesky | solution.py:18
  505.6 9.8 custom-call.15
  515.9 11.7 %cholesky.189 = f32[128,128]{1,0:T(8,128)S(1)} custom-call(f32[128,128]{1,0:T(8,128)S(1)} %convolution_subtract_fusion.5), custom_call_target="Cholesky" | custom-call | tf_op jit(solution)/shard_map/jit(cholesky)/cholesky | solution.py:18
  529.7 4.3 while.9
  530.6 1.3 bitcast_dynamic-update-slice_fusion.6
  532.6 1.3 bitcast_dynamic-update-slice_fusion.6
  534.0 19.7 %custom-call.16 = f32[2,128,128]{1,2,0:T(8,128)S(1)} custom-call(f32[2,128,128]{2,1,0:T(8,128)S(1)} %get-tuple-element.63), custom_call_target="InvertDiagBlocksLowerTriangular" | custom-call | tf_op jit(solution)/shard_map/jit(_solve_triangular)/triangular_solve | solution.py:20
  554.6 1.4 fusion.25
  556.0 1.1 fusion.13
  557.8 50.5 %all-gather.4.cloned.1.call-done = bf16[8192,256]{1,0:T(8,128)(2,1)} async-done(((bf16[512,256]{1,0:T(8,128)(2,1)}), bf16[8192,256]{1,0:T(8,128)(2,1)}) %all-gather.4.cloned.1.call-update) | async-done | bytes 4194320 | tf_op jit(solution)/shard_map/all_gather | solution.py:113
  608.3 14.4 %fusion.1 = bf16[512,8192]{1,0:T(8,128)(2,1)} fusion(bf16[512,8192]{1,0:T(8,128)(2,1)} %copy-done.3, bf16[512,256]{1,0:T(8,128)(2,1)} %fusion.13, bf16[8192,256]{1,0:T(8,128)(2,1)} %all-gather.4.cloned.1.call-done, pred[512]{0:T(512)(128)(4,1)S(1)} %fusion.103, pred[8192]{0:T(1024)(128)(4,1)S(1)} %iota_compare_fusion.15), kind=kOutput, calls=%fused_computation.16 | convolution fusion | flops 2168455168 | bytes 21242368 | tf_op jit(solution)/shard_map/dot_general | solution.py:42
  622.7 2.3 fusion.24
  625.0 2.0 fusion.19
  627.5 86.9 %all-reduce.7.cloned.1.call-done = f32[256,256]{0,1:T(8,128)} async-done(((f32[256,256]{0,1:T(8,128)}), f32[256,256]{0,1:T(8,128)}) %all-reduce.7.cloned.1.call-update) | async-done | bytes 262160 | tf_op jit(solution)/shard_map/psum | solution.py:102
  716.5 11.7 %cholesky.206 = f32[128,128]{1,0:T(8,128)S(1)} custom-call(f32[128,128]{1,0:T(8,128)S(1)} %cholesky.273), custom_call_target="Cholesky" | custom-call | tf_op jit(solution)/shard_map/jit(cholesky)/cholesky | solution.py:18
  728.3 9.8 custom-call.17
  738.6 11.7 %cholesky.223 = f32[128,128]{1,0:T(8,128)S(1)} custom-call(f32[128,128]{1,0:T(8,128)S(1)} %convolution_subtract_fusion.4), custom_call_target="Cholesky" | custom-call | tf_op jit(solution)/shard_map/jit(cholesky)/cholesky | solution.py:18
  753.0 4.2 while.10
  753.8 1.3 bitcast_dynamic-update-slice_fusion.7
  755.9 1.3 bitcast_dynamic-update-slice_fusion.7
  757.2 19.7 %custom-call.18 = f32[2,128,128]{1,2,0:T(8,128)S(1)} custom-call(f32[2,128,128]{2,1,0:T(8,128)S(1)} %get-tuple-element.64), custom_call_target="InvertDiagBlocksLowerTriangular" | custom-call | tf_op jit(solution)/shard_map/jit(_solve_triangular)/triangular_solve | solution.py:20
  777.8 1.4 fusion.29
  779.2 1.1 fusion.14
  781.1 50.5 %all-gather.6.cloned.1.call-done = bf16[8192,256]{1,0:T(8,128)(2,1)} async-done(((bf16[512,256]{1,0:T(8,128)(2,1)}), bf16[8192,256]{1,0:T(8,128)(2,1)}) %all-gather.6.cloned.1.call-update) | async-done | bytes 4194320 | tf_op jit(solution)/shard_map/all_gather | solution.py:113
  831.6 14.4 %fusion.3 = bf16[512,8192]{1,0:T(8,128)(2,1)} fusion(bf16[512,8192]{1,0:T(8,128)(2,1)} %fusion.24, bf16[512,256]{1,0:T(8,128)(2,1)} %fusion.14, bf16[8192,256]{1,0:T(8,128)(2,1)} %all-gather.6.cloned.1.call-done, pred[512]{0:T(512)(128)(4,1)S(1)} %fusion.104, pred[8192]{0:T(1024)(128)(4,1)S(1)} %iota_compare_fusion.16), kind=kOutput, calls=%fused_computation.18 | convolution fusion | flops 2168455168 | bytes 21242368 | tf_op jit(solution)/shard_map/dot_general | solution.py:42
  845.9 2.3 fusion.23
  848.2 2.0 fusion.17
  850.5 87.1 %all-reduce.9.cloned.1.call-done = f32[256,256]{0,1:T(8,128)} async-done(((f32[256,256]{0,1:T(8,128)}), f32[256,256]{0,1:T(8,128)}) %all-reduce.9.cloned.1.call-update) | async-done | bytes 262160 | tf_op jit(solution)/shard_map/psum | solution.py:102
  939.8 11.7 %cholesky.240 = f32[128,128]{1,0:T(8,128)S(1)} custom-call(f32[128,128]{1,0:T(8,128)S(1)} %cholesky.276), custom_call_target="Cholesky" | custom-call | tf_op jit(solution)/shard_map/jit(cholesky)/cholesky | solution.py:18
  951.5 9.8 custom-call.19
  961.8 11.7 %cholesky.257 = f32[128,128]{1,0:T(8,128)S(1)} custom-call(f32[128,128]{1,0:T(8,128)S(1)} %convolution_subtract_fusion.3), custom_call_target="Cholesky" | custom-call | tf_op jit(solution)/shard_map/jit(cholesky)/cholesky | solution.py:18
  976.2 4.3 while.11
  977.2 1.3 bitcast_dynamic-update-slice_fusion.8
  979.2 1.3 bitcast_dynamic-update-slice_fusion.8
  980.6 19.7 %custom-call.20 = f32[2,128,128]{1,2,0:T(8,128)S(1)} custom-call(f32[2,128,128]{2,1,0:T(8,128)S(1)} %get-tuple-element.65), custom_call_target="InvertDiagBlocksLowerTriangular" | custom-call | tf_op jit(solution)/shard_map/jit(_solve_triangular)/triangular_solve | solution.py:20
  1001.2 1.4 fusion.33
  1002.5 1.1 fusion.15
  1004.4 50.5 %all-gather.8.cloned.1.call-done = bf16[8192,256]{1,0:T(8,128)(2,1)} async-done(((bf16[512,256]{1,0:T(8,128)(2,1)}), bf16[8192,256]{1,0:T(8,128)(2,1)}) %all-gather.8.cloned.1.call-update) | async-done | bytes 4194320 | tf_op jit(solution)/shard_map/all_gather | solution.py:113
  1054.9 14.2 %fusion.5 = bf16[512,8192]{1,0:T(8,128)(2,1)} fusion(bf16[512,8192]{1,0:T(8,128)(2,1)} %fusion.23, bf16[512,256]{1,0:T(8,128)(2,1)} %fusion.15, bf16[8192,256]{1,0:T(8,128)(2,1)} %all-gather.8.cloned.1.call-done, pred[512]{0:T(512)(128)(4,1)S(1)} %fusion.105, pred[8192]{0:T(1024)(128)(4,1)S(1)} %iota_compare_fusion.17), kind=kOutput, calls=%fused_computation.20 | convolution fusion | flops 2168455168 | bytes 21242368 | tf_op jit(solution)/shard_map/dot_general | solution.py:42
  1069.1 7.8 copy.100
  1076.9 2.4 fusion.22
  (114 shorter events, 24.5 us)
Async XLA Ops:
  6.5 19.9 %copy-start = (s32[4,64]{1,0:T(4,128)S(1)}, s32[4,64]{1,0:T(4,128)}, u32[]{:S(2)}) copy-start(s32[4,64]{1,0:T(4,128)} %param.20) | copy-start | bytes 3076
  12.4 14.6 %copy-start.2 = (s32[4]{0:T(128)S(1)}, s32[4]{0:T(128)}, u32[]{:S(2)}) copy-start(s32[4]{0:T(128)} %param.19) | copy-start | bytes 52
  22.8 48.9 %collective-permute-start = (bf16[256,4096]{0,1:T(8,128)(2,1)}, bf16[256,4096]{0,1:T(8,128)(2,1)}, u32[]{:S(2)}, u32[]{:S(2)}) collective-permute-start(bf16[256,4096]{0,1:T(8,128)(2,1)} %get-tuple-element.97), channel_id=1, source_target_pairs={{0,16},{16,0},{1,17},{17,1},{2,18},{18,2},{3,19},{19,3},{4,20},{20... | collective-permute-start | bytes 6291464 | tf_op jit(solution)/shard_map/ppermute | solution.py:14
  107.0 6.7 copy-start.8
  107.0 157.1 %all-to-all-start = ((bf16[2,256,8192]{1,0,2:T(2,128)(2,1)}), bf16[2,256,8192]{1,0,2:T(2,128)(2,1)}, u32[]{:S(2)}, u32[]{:S(2)}) async-start(bf16[2,256,8192]{1,0,2:T(2,128)(2,1)} %copy.48), calls=%async_computation | async-start | bytes 16777216 | tf_op jit(solution)/shard_map/all_to_all | solution.py:83
  113.4 378.3 %all-reduce.5.cloned.1.call-start = ((), (), s32[]{:S(2)}) async-start(), calls=%async_computation.1 | async-start | bytes 524288 | tf_op jit(solution)/shard_map/psum | solution.py:102
  330.4 26.4 %copy-start.7 = (f32[1,512]{1,0:T(1,128)S(1)}, f32[1,512]{1,0:T(1,128)}, u32[]{:S(2)}) copy-start(f32[1,512]{1,0:T(1,128)} %param.15) | copy-start | bytes 6148
  366.5 3.4 copy-start.3
  370.9 237.4 %all-gather.4.cloned.1.call-start = ((), (), s32[]{:S(2)}) async-start(), calls=%async_computation.2 | async-start | bytes 4456448 | tf_op jit(solution)/shard_map/all_gather | solution.py:113
  557.1 157.3 %all-reduce.7.cloned.1.call-start = ((), (), s32[]{:S(2)}) async-start(), calls=%async_computation.3 | async-start | bytes 524288 | tf_op jit(solution)/shard_map/psum | solution.py:102
  557.8 64.9 %copy-start.6 = (bf16[512,256]{1,0:T(8,128)(2,1)S(1)}, bf16[512,256]{1,0:T(8,128)(2,1)}, u32[]{:S(2)}) copy-start(bf16[512,256]{1,0:T(8,128)(2,1)} %fusion.13) | copy-start | bytes 786436
  627.0 204.5 %all-gather.6.cloned.1.call-start = ((), (), s32[]{:S(2)}) async-start(), calls=%async_computation.4 | async-start | bytes 4456448 | tf_op jit(solution)/shard_map/all_gather | solution.py:113
  780.3 157.3 %all-reduce.9.cloned.1.call-start = ((), (), s32[]{:S(2)}) async-start(), calls=%async_computation.5 | async-start | bytes 524288 | tf_op jit(solution)/shard_map/psum | solution.py:102
  781.1 64.9 %copy-start.4 = (bf16[512,256]{1,0:T(8,128)(2,1)S(1)}, bf16[512,256]{1,0:T(8,128)(2,1)}, u32[]{:S(2)}) copy-start(bf16[512,256]{1,0:T(8,128)(2,1)} %fusion.14) | copy-start | bytes 786436
  850.2 204.7 %all-gather.8.cloned.1.call-start = ((), (), s32[]{:S(2)}) async-start(), calls=%async_computation.6 | async-start | bytes 4456448 | tf_op jit(solution)/shard_map/all_gather | solution.py:113
  1069.1 10.2 copy-start.1
  1069.1 7.8 copy-start.5
Sparse Core Ops, SparseCore 0:
  371.0 120.6 all-reduce.4
  557.2 51.0 all-gather.3
  627.1 87.2 all-reduce.6
  780.5 51.0 all-gather.5
  850.4 87.2 all-reduce.8
  1003.8 51.0 all-gather.7
where the time goes:
time: 1100 us; the launch traced here: 1090 us
  waiting for transfers between devices  638 us (58%)
  other arithmetic  196 us (18%)
  local copies, waits for them, and re-layouts  138 us (13%)
  matrix products  83.9 us (8%)
  between operations  20 us (2%)
    psum x3, waiting for transfers between devices, body(): lax.psum(pivot_rows(matrix[:, left_edge:right_edge], row_ids, left_edge),...  295 us
    all_gather x3, waiting for transfers between devices, body(): lax.all_gather(own_factor, 'grid', axis=0, tiled=True)  151 us
    all_to_all x1, waiting for transfers between devices, body(): lax.all_to_all(spread, 'grid', split_axis=2, concat_axis=1, tiled=True)  149 us
    another operation x20, other arithmetic, pivot_parts(): pivot_factor = jnp.linalg.cholesky(pivot_block)  103 us
    another operation x7, other arithmetic, pivot_parts(): jax.scipy.linalg.solve_triangular(pivot_factor, identity, lower=True)  59.1 us
    add x2, local copies, waits for them, and re-layouts, body(): summed = placed[0].astype(jnp.float32) + placed[1].astype(jnp.float32)  45.9 us
    dot_general x3, matrix products, renew(): lax.dot_general(own_factor, portion, (((1,), (1,)), ((), ())), preferred_...  42.9 us
    ppermute x1, waiting for transfers between devices, swapped(): return lax.ppermute(value, axis, pairs)  42.8 us
  transfers between devices with their start and end apart: 8, of which 8 were waited for; matrix products, arithmetic and copies ran while one was open for 0% of the time, Pallas kernels for 0%

commit v1 on v0

v1 whole, which is shorter than its diff:
```python
import functools
import jax
import jax.numpy as jnp
from jax import lax
from jax.experimental import pallas as pl
from jax.experimental.pallas import tpu as pltpu
from jax.sharding import PartitionSpec as P

BLK = 64
PW = 256
PANELS = 3
TOP = PW * PANELS
UNIT = PW // BLK
F32 = jnp.float32
BF16 = jnp.bfloat16
VMEM_LIMIT = 56 * 1024 * 1024


def swapped(value, axis, distance):
    mask = 2**distance
    pairs = [(source, source ^ mask) for source in range(lax.axis_size(axis))]
    return lax.ppermute(value, axis, pairs)


def pivot_parts(pivot_block):
    pivot_factor = jnp.linalg.cholesky(pivot_block)
    identity = jnp.eye(PW, dtype=F32)
    pivot_inverse = jax.scipy.linalg.solve_triangular(pivot_factor, identity, lower=True)
    return (pivot_factor, pivot_inverse)


def split3(value):
    hi = value.astype(BF16)
    rest = value - hi.astype(F32)
    mid = rest.astype(BF16)
    return hi, mid, (rest - mid.astype(F32)).astype(BF16)


def dot_nt(a, b):
    return lax.dot_general(a, b, (((1,), (1,)), ((), ())), preferred_element_type=F32)


def spread_kernel(lane_start, src_ref, child_ref, out_ref, *, window):
    start = pl.multiple_of(lane_start[pl.program_id(0)] * 128, 128)
    ids = lax.broadcasted_iota(jnp.int32, (window, src_ref.shape[1]), 0)
    pick = (ids == src_ref[...] - start).astype(F32).astype(BF16)
    values = child_ref[:, pl.ds(start, window)]
    out_ref[0] = jnp.dot(values, pick, preferred_element_type=F32).astype(BF16)


def spread(child, lane_start, source_cols, grid_size, window):
    child_rows, child_order = child.shape
    rows_here = source_cols.shape[1] // grid_size
    return pl.pallas_call(
        functools.partial(spread_kernel, window=window),
        grid_spec=pltpu.PrefetchScalarGridSpec(
            num_scalar_prefetch=1,
            grid=(grid_size,),
            in_specs=[
                pl.BlockSpec((1, rows_here), lambda t, s: (0, t)),
                pl.BlockSpec((child_rows, child_order), lambda t, s: (0, 0)),
            ],
            out_specs=pl.BlockSpec((1, child_rows, rows_here), lambda t, s: (t, 0, 0)),
        ),
        out_shape=jax.ShapeDtypeStruct((grid_size, child_rows, rows_here), BF16),
        compiler_params=pltpu.CompilerParams(vmem_limit_bytes=VMEM_LIMIT),
        cost_estimate=pl.CostEstimate(
            flops=2 * child_rows * window * source_cols.shape[1],
            bytes_accessed=6 * child_rows * source_cols.shape[1],
            transcendentals=0,
        ),
    )(lane_start, source_cols, child)


def panels_kernel(inverse, c0, c1, c2, place, factors, solves, crosses, out_ref, parts):
    tile = pl.program_id(0)
    blocks = inverse.shape[0] // 2

    @pl.when(tile == 0)
    def _():
        for step in range(PANELS):
            for index, part in enumerate(split3(solves[step])):
                parts[step, index] = part

    rows = []
    for child in range(2):
        picked = []
        for chunk in (c0, c1, c2):
            pieces = []
            for unit in range(UNIT):
                block = inverse[child * blocks + tile * UNIT + unit]
                at = pl.multiple_of(jnp.maximum(block, 0) * BLK, BLK)
                piece = chunk[pl.ds(at, BLK), child * PW : (child + 1) * PW].astype(F32)
                pieces.append(jnp.where(block >= 0, piece, 0.0).astype(BF16))
            picked.append(jnp.concatenate(pieces, axis=0))
        rows.append(picked)
    done = []
    for step in range(PANELS):
        low, high = step * PW, (step + 1) * PW
        total = jnp.zeros((PW, PW), F32)
        for child in range(2):
            for chunk in range(step + 1):
                total += jnp.dot(
                    rows[child][chunk],
                    place[child, chunk * PW : (chunk + 1) * PW, low:high],
                    preferred_element_type=F32,
                )
        current = total.astype(BF16)
        for earlier in range(step):
            cross = crosses[low:high, earlier * PW : (earlier + 1) * PW]
            current = (current.astype(F32) - dot_nt(done[earlier], cross)).astype(BF16)
        solved = dot_nt(current, parts[step, 2]) + dot_nt(current, parts[step, 1])
        solved = solved + dot_nt(current, parts[step, 0])
        chosen = jnp.where(tile == step, factors[step], solved)
        chosen = jnp.where(tile < step, 0.0, chosen).astype(BF16)
        done.append(chosen)
        out_ref[:, low:high] = chosen


def panels(inverse, chunks, place, factors, solves, crosses, front_order):
    whole = lambda shape: pl.BlockSpec(shape, lambda t, s: (0,) * len(shape))
    return pl.pallas_call(
        panels_kernel,
        grid_spec=pltpu.PrefetchScalarGridSpec(
            num_scalar_prefetch=1,
            grid=(front_order // PW,),
            in_specs=[whole(x.shape) for x in (*chunks, place, factors, solves, crosses)],
            out_specs=pl.BlockSpec((PW, TOP), lambda t, s: (t, 0)),
            scratch_shapes=[pltpu.VMEM((PANELS, 3, PW, PW), BF16)],
        ),
        out_shape=jax.ShapeDtypeStruct((front_order, TOP), BF16),
        compiler_params=pltpu.CompilerParams(vmem_limit_bytes=VMEM_LIMIT),
    )(inverse, *chunks, place, factors, solves, crosses)


def trailing_kernel(scalars, src_ref, diag_ref, own_ref, far_ref, mine_ref, tile_ref, out_ref):
    tile = pl.program_id(0)
    rows_here = out_ref.shape[0]
    tiles = pl.num_programs(0)
    active, first_row = scalars[2 * tiles], scalars[2 * tiles + 1]

    @pl.when(tile < PANELS)
    def _():
        for step in range(PANELS):
            @pl.when(tile == step)
            def _():
                out_ref[...] = mine_ref[:, step * PW : (step + 1) * PW]

    @pl.when(tile >= PANELS)
    def _():
        ids = lax.broadcasted_iota(jnp.int32, (PW, PW), 0)
        total = None
        for child, ref in enumerate((own_ref, far_ref)):
            start = pl.multiple_of(scalars[child * tiles + tile] * BLK, BLK)
            pick = (ids == src_ref[child : child + 1, :] - start).astype(F32).astype(BF16)
            term = lax.dot_general(
                ref[pl.ds(start, PW), :], pick, (((0,), (0,)), ((), ())),
                preferred_element_type=F32,
            )
            total = term if total is None else total + term
        row = first_row + lax.broadcasted_iota(jnp.int32, (rows_here, PW), 0)
        col = tile * PW + lax.broadcasted_iota(jnp.int32, (rows_here, PW), 1)
        on_diag = row == col
        total = total + jnp.where(on_diag, diag_ref[...], 0.0)
        padding = (row >= active) | (col >= active)
        current = jnp.where(padding, jnp.where(on_diag, 1.0, 0.0), total).astype(BF16)
        for step in range(PANELS):
            low, high = step * PW, (step + 1) * PW
            product = dot_nt(mine_ref[:, low:high], tile_ref[:, low:high])
            current = (current.astype(F32) - product).astype(BF16)
        out_ref[...] = jnp.where(row < TOP, 0.0, current.astype(F32)).astype(BF16)


def trailing(scalars, source_rows, diag, own, far, mine, factor):
    front_order = factor.shape[0]
    rows_here = mine.shape[0]
    tiles = front_order // PW
    whole = lambda x: pl.BlockSpec(x.shape, lambda t, s: (0,) * x.ndim)
    return pl.pallas_call(
        trailing_kernel,
        grid_spec=pltpu.PrefetchScalarGridSpec(
            num_scalar_prefetch=1,
            grid=(tiles,),
            in_specs=[
                pl.BlockSpec((2, PW), lambda t, s: (0, t)),
                whole(diag), whole(own), whole(far), whole(mine),
                pl.BlockSpec((PW, TOP), lambda t, s: (t, 0)),
            ],
            out_specs=pl.BlockSpec((rows_here, PW), lambda t, s: (0, t)),
        ),
        out_shape=jax.ShapeDtypeStruct((rows_here, front_order), BF16),
        compiler_params=pltpu.CompilerParams(vmem_limit_bytes=VMEM_LIMIT),
    )(scalars, source_rows, diag, own, far, mine, factor)


def highest(a, b):
    return jnp.dot(a.astype(F32), b, precision=lax.Precision.HIGHEST)


def pivot_chain(tops):
    factors, inverses, rows_of = [], [], []
    for step in range(PANELS):
        low = step * PW
        current = tops[step][low:]
        for earlier in range(step):
            lower = rows_of[earlier][low:]
            product = dot_nt(lower, lower[:PW])
            current = (current.astype(F32) - product).astype(BF16)
        factor, inverse = pivot_parts(current[:PW].astype(F32))
        factors.append(factor)
        inverses.append(inverse)
        below = highest(current[PW:], inverse.T).astype(BF16)
        head = jnp.zeros((low + PW, PW), BF16)
        rows_of.append(jnp.concatenate([head, below], axis=0))
    return jnp.stack(factors), jnp.stack(inverses), jnp.concatenate(rows_of, axis=1)


def body(front_diag, children, parent, front_blocks, child_blocks, row_map):
    leaf_id = lax.axis_index("leaf")
    grid_id = lax.axis_index("grid")
    grid_size = lax.axis_size("grid")
    rows_here = front_diag.shape[1]
    front_order = rows_here * grid_size
    child_order = children.shape[2]
    blocks_front = front_order // BLK
    blocks_child = child_order // BLK
    partner = jnp.bitwise_xor(leaf_id, 1)
    first_child = 2 * leaf_id
    keep_first = parent[first_child] == leaf_id
    own_child = jnp.where(keep_first, first_child, first_child + 1)
    partner_first = 2 * partner
    far_child = jnp.where(parent[partner_first] == leaf_id, partner_first, partner_first + 1)
    own_part = jnp.where(keep_first, children[0], children[1])
    away_part = jnp.where(keep_first, children[1], children[0])

    strip_far = swapped(away_part[:, :TOP], "leaf", 0)
    arrived = swapped(away_part, "leaf", 0)
    diag_all = lax.all_gather(front_diag[0], "grid", axis=0, tiled=True)
    chunks = []
    for step in range(PANELS):
        low, high = step * PW, (step + 1) * PW
        pair = jnp.concatenate([own_part[:, low:high], strip_far[:, low:high]], axis=1)
        chunks.append(lax.all_gather(pair, "grid", axis=0, tiled=True))

    ids = jnp.stack([own_child, far_child])
    maps = row_map[ids]
    live = jnp.arange(blocks_child)[None, :] < child_blocks[ids][:, None]
    hits = (maps[:, :, None] == jnp.arange(blocks_front)[None, None, :]) & live[:, :, None]
    inverse = jnp.max(jnp.where(hits, jnp.arange(blocks_child)[None, :, None], -1), axis=1)
    source = jnp.where(
        inverse[:, :, None] >= 0, inverse[:, :, None] * BLK + jnp.arange(BLK), -(2**20)
    ).reshape(2, front_order).astype(jnp.int32)
    filled = (inverse >= 0).astype(jnp.int32)
    before = jnp.cumsum(filled, axis=1) - filled
    per_device = rows_here // BLK
    window = (per_device + 2) * BLK
    lane_start = jnp.minimum(before[:, ::per_device] // 2, (child_order - window) // 128)
    row_start = jnp.minimum(before[:, ::UNIT], blocks_child - UNIT)

    own_spread = spread(own_part, lane_start[0], source[0:1], grid_size, window)
    own_rows = lax.all_to_all(own_spread, "grid", split_axis=0, concat_axis=0, tiled=True)
    far_spread = spread(arrived, lane_start[1], source[1:2], grid_size, window)
    far_rows = lax.all_to_all(far_spread, "grid", split_axis=0, concat_axis=0, tiled=True)

    place = (jnp.arange(TOP)[None, :, None] == source[:, None, :TOP]).astype(BF16)
    tops = []
    for step in range(PANELS):
        low, high = step * PW, (step + 1) * PW
        total = jnp.zeros((TOP, PW), F32)
        for child in range(2):
            part = jnp.zeros((TOP, PW), F32)
            for chunk in range(step + 1):
                rows = chunks[chunk][:TOP, child * PW : (child + 1) * PW]
                part = part + jnp.dot(
                    rows, place[child, chunk * PW : (chunk + 1) * PW, low:high],
                    preferred_element_type=F32,
                )
            total = total + lax.dot_general(
                place[child], part.astype(BF16), (((0,), (0,)), ((), ())),
                preferred_element_type=F32,
            )
        shifted = jnp.arange(TOP)[:, None] == jnp.arange(low, high)[None, :]
        total = total + jnp.where(shifted, diag_all[:TOP, None], 0.0)
        tops.append(total.astype(BF16))
    factors, inverses, crosses = pivot_chain(tops)
    factor = panels(
        inverse.reshape(-1).astype(jnp.int32), chunks, place, factors, inverses, crosses, front_order
    )
    mine = lax.dynamic_slice_in_dim(factor, grid_id * rows_here, rows_here, axis=0)
    scalars = jnp.concatenate(
        [row_start.reshape(-1), (front_blocks[leaf_id] * BLK)[None], (grid_id * rows_here)[None]]
    ).astype(jnp.int32)
    matrix = trailing(
        scalars, source, front_diag[0][:, None],
        own_rows.reshape(child_order, rows_here), far_rows.reshape(child_order, rows_here),
        mine, factor,
    )
    return matrix[None]


def solution(mesh):
    in_specs = (P("leaf", "grid"), P("leaf", "grid", None), P(), P(), P(), P())
    out_specs = P("leaf", "grid", None)
    return jax.shard_map(body, mesh=mesh, in_specs=in_specs, out_specs=out_specs, check_vma=False)
```

time: 1100 us -> 538 us (0.49)
  waiting for transfers between devices: 638 us -> 8.52 us
  local copies, waits for them, and re-layouts: 138 us -> 24 us
  blocking collectives: 0 us -> 109 us
  Pallas kernels: 0 us -> 107 us
  matrix products: 83.9 us -> 36 us
  starting transfers between devices: 10.4 us -> 50.4 us
  other arithmetic: 196 us -> 178 us
    psum x3 -> x0, waiting for transfers between devices: 295 us -> none  [body(): lax.psum(pivot_rows(matrix[:, left_edge:right_edge], row_ids, left_edge),...]
    all_gather x3, waiting for transfers between devices: 151 us -> 0.02 us  [body(): chunks.append(lax.all_gather(pair, 'grid', axis=0, tiled=True))]
    all_to_all x1 -> x2, waiting for transfers between devices: 149 us -> 0.01 us  [the longest x1 0.01 us: body(): lax.all_to_all(own_spread, 'grid', split_axis=0, concat_axis=0, tiled=True)]
    all_gather x0 -> x1, blocking collectives: none -> 109 us  [body(): diag_all = lax.all_gather(front_diag[0], 'grid', axis=0, tiled=True)]
    pallas_call x0 -> x4, Pallas kernels: none -> 107 us  [the longest x1 50.7 us: panels(): pl.pallas_call(panels_kernel, grid_spec=pltpu.PrefetchScalarGridSpec(num_...]
    dot_general x14 -> x17, matrix products: 79.9 us -> 31.9 us  [the longest x6 17 us: body(): lax.dot_general(place[child], part.astype(BF16), (((0,), (0,)), ((), ()))...]
    add x2 -> x4, local copies, waits for them, and re-layouts: 45.9 us -> 0.29 us  [body(): inverse[:, :, None] * BLK + jnp.arange(BLK)]
    all_to_all x1 -> x2, starting transfers between devices: 6.38 us -> 45.5 us  [the longest x1 39.3 us: body(): lax.all_to_all(far_spread, 'grid', split_axis=0, concat_axis=0, tiled=True)]
  transfers between devices with their start and end apart: 8 -> 7, of which waited for: 8 -> 1; matrix products, arithmetic and copies ran while one was open for 0% -> 44% of each run, Pallas kernels for 0% -> 14%
where the time goes in v1:
time: 538 us; the launch traced here: 532 us
  other arithmetic  178 us (33%)
  blocking collectives  109 us (20%)
  Pallas kernels  107 us (20%)
  starting transfers between devices  50.4 us (9%)
  matrix products  36 us (7%)
  local copies, waits for them, and re-layouts  24 us (4%)
  between operations  19.7 us (4%)
  waiting for transfers between devices  8.52 us (2%)
    all_gather x1, blocking collectives, body(): diag_all = lax.all_gather(front_diag[0], 'grid', axis=0, tiled=True)  109 us
    another operation x20, other arithmetic, pivot_parts(): pivot_factor = jnp.linalg.cholesky(pivot_block)  104 us
    another operation x5, other arithmetic, pivot_parts(): jax.scipy.linalg.solve_triangular(pivot_factor, identity, lower=True)  59.6 us
    pallas_call x1, Pallas kernels, panels(): pl.pallas_call(panels_kernel, grid_spec=pltpu.PrefetchScalarGridSpec(num_...  50.7 us
    all_to_all x1, starting transfers between devices, body(): lax.all_to_all(far_spread, 'grid', split_axis=0, concat_axis=0, tiled=True)  39.3 us
    pallas_call x1, Pallas kernels, trailing(): pl.pallas_call(trailing_kernel, grid_spec=pltpu.PrefetchScalarGridSpec(nu...  31.8 us
    pallas_call x2, Pallas kernels, spread(): pl.pallas_call(functools.partial(spread_kernel, window=window), grid_spec...  24.4 us
    dot_general x6, matrix products, body(): lax.dot_general(place[child], part.astype(BF16), (((0,), (0,)), ((), ()))...  17 us
  transfers between devices with their start and end apart: 7, of which 1 were waited for; matrix products, arithmetic and copies ran while one was open for 44% of the time, Pallas kernels for 14%

profile of v1, /device:TPU:0, one launch (start us, length us, event | category | flops | bytes accessed | tf_op | source)
XLA Modules:
  0.0 532.0 jit_solution(16850414582945513658)
XLA Ops:
  6.5 1.4 fusion.97
  8.6 2.5 select_bitcast_fusion
  11.2 3.0 collective-permute-start.1
  14.2 0.7 fusion.94
  14.8 8.4 %collective-permute-done.1 = bf16[256,768]{1,0:T(8,128)(2,1)S(1)} collective-permute-done((bf16[256,768]{1,0:T(8,128)(2,1)S(1)}, bf16[256,768]{1,0:T(8,128)(2,1)S(1)}, u32[]{:S(2)}, u32[]{:S(2)}) %collective-permute-start.1) | collective-permute-done | bytes 393248 | tf_op jit(solution)/shard_map/ppermute | solution.py:22
  23.3 0.7 fusion.95
  24.0 0.7 pad_maximum_fusion.2
  24.8 0.7 pad_maximum_fusion.3
  25.5 1.8 collective-permute-start
  30.1 0.7 slice.192.src_ref
  31.4 12.1 %shard_map.64 = bf16[16,256,512]{2,1,0:T(8,128)(2,1)} custom-call(s32[16]{0:T(128)} %get-tuple-element.93.lane_start, s32[1,8192]{1,0:T(1,128)} %slice.192.src_ref, bf16[256,4096]{1,0:T(8,128)(2,1)} %copy-done.3), custom_call_target="tpu_custom_call" | custom-call | flops 2684354560 | bytes 12582912 | tf_op jit(solution)/shard_map/pallas_call | solution.py:54
  43.4 6.1 %all-to-all-start = ((bf16[16,256,512]{2,1,0:T(8,128)(2,1)}), bf16[16,256,512]{2,1,0:T(8,128)(2,1)}, u32[]{:S(2)}, u32[]{:S(2)}) async-start(bf16[16,256,512]{2,1,0:T(8,128)(2,1)} %shard_map.64), calls=%async_computation | async-start | bytes 8388608 | tf_op jit(solution)/shard_map/all_to_all | solution.py:261
  50.3 108.8 %all-gather = f32[1,8192]{1,0:T(1,128)S(1)} all-gather(f32[1,512]{1,0:T(1,128)S(1)} %copy-done.6), channel_id=2, replica_groups=mesh['leaf'=2,'grid'=16] {'grid'}, dimensions={1}, use_global_device_ids=true | all-gather | bytes 34816 | tf_op jit(solution)/shard_map/all_gather | solution.py:238
  160.9 0.7 slice.197.src_ref
  161.7 0.9 copy.50.diag_ref
  165.6 2.6 iota_compare_fusion
  168.2 1.7 pad_maximum_fusion.4
  169.9 12.3 %shard_map.65 = bf16[16,256,512]{2,1,0:T(8,128)(2,1)} custom-call(s32[16]{0:T(128)} %get-tuple-element.92.lane_start, s32[1,8192]{1,0:T(1,128)} %slice.197.src_ref, bf16[256,4096]{1,0:T(8,128)(2,1)} %collective-permute-done.child_ref), custom_call_target="tpu_custom_call" | custom-call | flops 2684354560 | bytes 12582912 | tf_op jit(solution)/shard_map/pallas_call | solution.py:54
  182.3 2.1 fusion.11
  184.3 2.1 fusion.8
  186.6 11.7 %cholesky.172 = f32[128,128]{1,0:T(8,128)S(1)} custom-call(f32[128,128]{1,0:T(8,128)S(1)} %cholesky.270), custom_call_target="Cholesky" | custom-call | tf_op jit(solution)/shard_map/jit(cholesky)/cholesky | solution.py:26
  198.4 9.8 %custom-call.15 = f32[1,128,128]{1,2,0:T(8,128)S(1)} custom-call(f32[1,128,128]{2,1,0:T(8,128)S(1)} %get-tuple-element.89), custom_call_target="InvertDiagBlocksLowerTriangular" | custom-call | tf_op jit(solution)/shard_map/jit(cholesky)/cholesky | solution.py:26
  208.7 12.1 %cholesky.189 = f32[128,128]{1,0:T(8,128)S(1)} custom-call(f32[128,128]{1,0:T(8,128)S(1)} %convolution_subtract_fusion.8), custom_call_target="Cholesky" | custom-call | tf_op jit(solution)/shard_map/jit(cholesky)/cholesky | solution.py:26
  220.8 0.7 compare_reduce_fusion.4
  222.9 3.8 while.6
  223.5 1.3 bitcast_dynamic-update-slice_fusion.6
  225.4 1.3 bitcast_dynamic-update-slice_fusion.6
  226.7 19.7 %custom-call.16 = f32[2,128,128]{1,2,0:T(8,128)S(1)} custom-call(f32[2,128,128]{2,1,0:T(8,128)S(1)} %get-tuple-element.27), custom_call_target="InvertDiagBlocksLowerTriangular" | custom-call | tf_op jit(solution)/shard_map/jit(_solve_triangular)/triangular_solve | solution.py:28
  247.7 2.2 fusion.41
  249.9 2.2 fusion.35
  252.1 3.2 fusion.10
  255.4 3.2 fusion.13
  258.6 1.5 fusion.14
  260.3 11.7 %cholesky.206 = f32[128,128]{1,0:T(8,128)S(1)} custom-call(f32[128,128]{1,0:T(8,128)S(1)} %cholesky.273), custom_call_target="Cholesky" | custom-call | tf_op jit(solution)/shard_map/jit(cholesky)/cholesky | solution.py:26
  272.0 9.8 %custom-call.17 = f32[1,128,128]{1,2,0:T(8,128)S(1)} custom-call(f32[1,128,128]{2,1,0:T(8,128)S(1)} %get-tuple-element.85), custom_call_target="InvertDiagBlocksLowerTriangular" | custom-call | tf_op jit(solution)/shard_map/jit(cholesky)/cholesky | solution.py:26
  282.3 11.9 %cholesky.223 = f32[128,128]{1,0:T(8,128)S(1)} custom-call(f32[128,128]{1,0:T(8,128)S(1)} %convolution_subtract_fusion.7), custom_call_target="Cholesky" | custom-call | tf_op jit(solution)/shard_map/jit(cholesky)/cholesky | solution.py:26
  294.2 0.6 compare_reduce_fusion.2
  294.9 0.7 compare_reduce_fusion.3
  296.8 39.3 %all-to-all-start.1 = ((bf16[16,256,512]{2,1,0:T(8,128)(2,1)}), bf16[16,256,512]{2,1,0:T(8,128)(2,1)}, u32[]{:S(2)}, u32[]{:S(2)}) async-start(bf16[16,256,512]{2,1,0:T(8,128)(2,1)} %shard_map.65), calls=%async_computation.1 | async-start | bytes 8388608 | tf_op jit(solution)/shard_map/all_to_all | solution.py:263
  336.2 4.0 while.7
  336.8 1.4 bitcast_dynamic-update-slice_fusion.7
  338.8 1.4 bitcast_dynamic-update-slice_fusion.7
  340.2 19.7 %custom-call.18 = f32[2,128,128]{1,2,0:T(8,128)S(1)} custom-call(f32[2,128,128]{2,1,0:T(8,128)S(1)} %get-tuple-element.28), custom_call_target="InvertDiagBlocksLowerTriangular" | custom-call | tf_op jit(solution)/shard_map/jit(_solve_triangular)/triangular_solve | solution.py:28
  361.1 1.3 fusion.39
  362.4 1.3 fusion.33
  363.6 2.2 convolution_add_fusion.4
  365.8 2.1 convolution_add_fusion.2
  368.0 3.2 fusion.9
  371.2 3.2 fusion.12
  374.4 1.3 fusion.18
  376.1 11.7 %cholesky.240 = f32[128,128]{1,0:T(8,128)S(1)} custom-call(f32[128,128]{1,0:T(8,128)S(1)} %cholesky.276), custom_call_target="Cholesky" | custom-call | tf_op jit(solution)/shard_map/jit(cholesky)/cholesky | solution.py:26
  387.9 9.8 %custom-call.19 = f32[1,128,128]{1,2,0:T(8,128)S(1)} custom-call(f32[1,128,128]{2,1,0:T(8,128)S(1)} %get-tuple-element.81), custom_call_target="InvertDiagBlocksLowerTriangular" | custom-call | tf_op jit(solution)/shard_map/jit(cholesky)/cholesky | solution.py:26
  398.2 11.9 %cholesky.257 = f32[128,128]{1,0:T(8,128)S(1)} custom-call(f32[128,128]{1,0:T(8,128)S(1)} %convolution_subtract_fusion.6), custom_call_target="Cholesky" | custom-call | tf_op jit(solution)/shard_map/jit(cholesky)/cholesky | solution.py:26
  410.1 0.7 compare_reduce_fusion
  412.9 4.1 while.8
  413.5 1.4 bitcast_dynamic-update-slice_fusion.8
  415.5 1.4 bitcast_dynamic-update-slice_fusion.8
  417.0 19.7 %custom-call.20 = f32[2,128,128]{1,2,0:T(8,128)S(1)} custom-call(f32[2,128,128]{2,1,0:T(8,128)S(1)} %get-tuple-element.29), custom_call_target="InvertDiagBlocksLowerTriangular" | custom-call | tf_op jit(solution)/shard_map/jit(_solve_triangular)/triangular_solve | solution.py:28
  437.7 0.9 pad_maximum_fusion.1.solves
  438.6 0.9 pad_maximum_fusion.factors
  439.5 1.1 fusion.16.crosses
  440.7 50.7 %shard_map.66.tile_ref = bf16[8192,768]{1,0:T(8,128)(2,1)} custom-call(s32[256]{0:T(256)} %bitcast.180, bf16[4096,512]{1,0:T(8,128)(2,1)} %all-gather.5.cloned.1.call-done.c0, bf16[4096,512]{1,0:T(8,128)(2,1)} %all-gather.7.cloned.1.call-done.c1, bf16[4096,512]{1,0:T(8,128)(2,1)} %all-gather.9.cloned.1.call-done.c2, ...), custom_call_target="tpu_custom_call" | custom-call | tf_op jit(solution)/shard_map/pallas_call | solution.py:122
  491.3 2.1 constant_dynamic-slice_fusion.3.mine_ref
  493.5 31.8 %shard_map.67 = bf16[512,8192]{1,0:T(8,128)(2,1)} custom-call(s32[66]{0:T(128)} %pad_add_fusion.scalars, s32[2,8192]{1,0:T(2,128)} %copy-done.4, f32[512,1]{1,0:T(8,128)} %copy.50.diag_ref, bf16[4096,512]{1,0:T(8,128)(2,1)} %bitcast.9.own_ref, bf16[4096,512]{1,0:T(8,128)(2,1)} %bitcast.12.far_ref, bf16[512,768]{1,0:T(8,128)(2,1)} %constant_dynamic-slice_fusion.3.mine_ref, ...), custom_call_target="tpu_custom_call" | custom-call | tf_op jit(solution)/shard_map/pallas_call | solution.py:179
  (137 shorter events, 18.1 us)
Async XLA Ops:
  6.5 21.6 %copy-start = (s32[4,64]{1,0:T(4,128)S(1)}, s32[4,64]{1,0:T(4,128)}, u32[]{:S(2)}) copy-start(s32[4,64]{1,0:T(4,128)} %param.14) | copy-start | bytes 3076
  6.5 175.7 %all-gather.5.cloned.1.call-start = ((), (), s32[]{:S(2)}) async-start(), calls=%async_computation.2 | async-start | bytes 4456448 | tf_op jit(solution)/shard_map/all_gather | solution.py:243
  11.1 3.1 copy-start.3
  11.1 17.6 %copy-start.2 = (s32[4]{0:T(128)S(1)}, s32[4]{0:T(128)}, u32[]{:S(2)}) copy-start(s32[4]{0:T(128)} %param.13) | copy-start | bytes 52
  11.2 12.1 %collective-permute-start.1 = (bf16[256,768]{1,0:T(8,128)(2,1)S(1)}, bf16[256,768]{1,0:T(8,128)(2,1)S(1)}, u32[]{:S(2)}, u32[]{:S(2)}) collective-permute-start(bf16[256,768]{1,0:T(8,128)(2,1)S(1)} %slice.258), channel_id=1, source_target_pairs={{0,16},{16,0},{1,17},{17,1},{2,18},{18,2},{3,19},{19,3},{4,20},{20... | collective-permute-start | bytes 1179656 | tf_op jit(solution)/shard_map/ppermute | solution.py:22
  24.7 227.4 %all-gather.7.cloned.1.call-start = ((), (), s32[]{:S(2)}) async-start(), calls=%async_computation.3 | async-start | bytes 4456448 | tf_op jit(solution)/shard_map/all_gather | solution.py:243
  25.5 144.4 %collective-permute-start = (bf16[256,4096]{1,0:T(8,128)(2,1)S(1)}, bf16[256,4096]{1,0:T(8,128)(2,1)}, u32[]{:S(2)}, u32[]{:S(2)}) collective-permute-start(bf16[256,4096]{1,0:T(8,128)(2,1)S(1)} %get-tuple-element.62), channel_id=1, source_target_pairs={{0,16},{16,0},{1,17},{17,1},{2,18},{18,2},{3,19},{19,3},{4,20},{20... | collective-permute-start | bytes 6291464 | tf_op jit(solution)/shard_map/ppermute | solution.py:22
  29.5 13.9 %copy-start.5 = (s32[2,128]{1,0:T(2,128)}, s32[2,128]{1,0:T(2,128)S(1)}, u32[]{:S(2)}) copy-start(s32[2,128]{1,0:T(2,128)S(1)} %select_reduce_fusion.6) | copy-start | bytes 3076
  43.4 6.8 %copy-start.6 = (f32[1,512]{1,0:T(1,128)S(1)}, f32[1,512]{1,0:T(1,128)}, u32[]{:S(2)}) copy-start(f32[1,512]{1,0:T(1,128)} %param.9) | copy-start | bytes 6148
  43.4 119.1 %copy-start.11 = (s32[2]{0:T(128)S(1)}, s32[2]{0:T(128)}, u32[]{:S(2)}) copy-start(s32[2]{0:T(128)} %param.12) | copy-start | bytes 28
  43.4 253.3 %all-to-all-start = ((bf16[16,256,512]{2,1,0:T(8,128)(2,1)}), bf16[16,256,512]{2,1,0:T(8,128)(2,1)}, u32[]{:S(2)}, u32[]{:S(2)}) async-start(bf16[16,256,512]{2,1,0:T(8,128)(2,1)} %shard_map.64), calls=%async_computation | async-start | bytes 8388608 | tf_op jit(solution)/shard_map/all_to_all | solution.py:261
  49.6 318.4 %all-gather.9.cloned.1.call-start = ((), (), s32[]{:S(2)}) async-start(), calls=%async_computation.4 | async-start | bytes 4456448 | tf_op jit(solution)/shard_map/all_gather | solution.py:243
  159.2 5.8 %copy-start.4 = (s32[2,8192]{1,0:T(2,128)}, s32[2,8192]{1,0:T(2,128)S(1)}, u32[]{:S(2)}) copy-start(s32[2,8192]{1,0:T(2,128)S(1)} %add_select_fusion.1.src_ref) | copy-start | bytes 196612
  186.4 36.4 %copy-start.12 = (s32[2]{0:T(128)S(1)}, s32[2]{0:T(128)}, u32[]{:S(2)}) copy-start(s32[2]{0:T(128)} %iota_multiply_fusion) | copy-start | bytes 28
  255.3 3.2 copy-start.7
  255.4 3.2 copy-start.10
  296.8 196.7 %all-to-all-start.1 = ((bf16[16,256,512]{2,1,0:T(8,128)(2,1)}), bf16[16,256,512]{2,1,0:T(8,128)(2,1)}, u32[]{:S(2)}, u32[]{:S(2)}) async-start(bf16[16,256,512]{2,1,0:T(8,128)(2,1)} %shard_map.65), calls=%async_computation.1 | async-start | bytes 8388608 | tf_op jit(solution)/shard_map/all_to_all | solution.py:263
  371.2 3.2 copy-start.8
  371.2 3.2 copy-start.9
  493.5 31.8 %copy-start.1 = (s32[4,64]{1,0:T(4,128)S(1)}, s32[4,64]{1,0:T(4,128)}, u32[]{:S(2)}) copy-start(s32[4,64]{1,0:T(4,128)} %param.14) | copy-start | bytes 3076
Sparse Core Ops, SparseCore 0:
  24.8 78.5 all-gather.4
  105.6 78.0 all-gather.6
  185.8 68.7 all-gather.8

commit v2 on v1

v2 whole, which is shorter than its diff:
```python
import functools
import jax
import jax.numpy as jnp
from jax import lax
from jax.experimental import pallas as pl
from jax.experimental.pallas import tpu as pltpu
from jax.sharding import PartitionSpec as P

BLK = 64
PW = 256
PANELS = 3
TOP = PW * PANELS
UNIT = PW // BLK
TILE = 512
EXTRA = 16
F32 = jnp.float32
BF16 = jnp.bfloat16
VMEM_LIMIT = 56 * 1024 * 1024


def swapped(value, axis, distance):
    mask = 2**distance
    pairs = [(source, source ^ mask) for source in range(lax.axis_size(axis))]
    return lax.ppermute(value, axis, pairs)


def highest(a, b):
    return jnp.dot(a.astype(F32), b, precision=lax.Precision.HIGHEST)


def rounded(value):
    return lax.reduce_precision(value, 8, 7)


def triangular_parts(block):
    factor = jnp.linalg.cholesky(block, symmetrize_input=False)
    identity = jnp.eye(block.shape[0], dtype=F32)
    return factor, jax.scipy.linalg.solve_triangular(factor, identity, lower=True)


def pivot_parts(pivot_block):
    half = PW // 2
    first, first_inverse = triangular_parts(pivot_block[:half, :half])
    cross = highest(pivot_block[half:, :half], first_inverse.T)
    second, second_inverse = triangular_parts(pivot_block[half:, half:] - highest(cross, cross.T))
    cross_inverse = -highest(second_inverse, highest(cross, first_inverse))
    zero = jnp.zeros((half, half), F32)
    pivot_factor = jnp.block([[first, zero], [cross, second]])
    pivot_inverse = jnp.block([[first_inverse, zero], [cross_inverse, second_inverse]])
    return (pivot_factor, pivot_inverse)


def split3(value):
    hi = value.astype(BF16)
    rest = value - hi.astype(F32)
    mid = rest.astype(BF16)
    return hi, mid, (rest - mid.astype(F32)).astype(BF16)


def dot_nt(a, b):
    return lax.dot_general(a, b, (((1,), (1,)), ((), ())), preferred_element_type=F32)


def spread_kernel(lane_start, src_ref, own_ref, far_ref, out_ref, *, window):
    ids = lax.broadcasted_iota(jnp.int32, (window, src_ref.shape[1]), 0)
    for child, ref in enumerate((own_ref, far_ref)):
        at = child * pl.num_programs(0) + pl.program_id(0)
        start = pl.multiple_of(lane_start[at] * 128, 128)
        pick = (ids == src_ref[child : child + 1, :] - start).astype(F32).astype(BF16)
        values = ref[:, pl.ds(start, window)]
        out_ref[0, child] = jnp.dot(values, pick, preferred_element_type=F32).astype(BF16)


def spread(own, far, lane_start, source_cols, grid_size, window):
    child_rows, child_order = own.shape
    rows_here = source_cols.shape[1] // grid_size
    return pl.pallas_call(
        functools.partial(spread_kernel, window=window),
        grid_spec=pltpu.PrefetchScalarGridSpec(
            num_scalar_prefetch=1,
            grid=(grid_size,),
            in_specs=[
                pl.BlockSpec((2, rows_here), lambda t, s: (0, t)),
                pl.BlockSpec((child_rows, child_order), lambda t, s: (0, 0)),
                pl.BlockSpec((child_rows, child_order), lambda t, s: (0, 0)),
            ],
            out_specs=pl.BlockSpec((1, 2, child_rows, rows_here), lambda t, s: (t, 0, 0, 0)),
        ),
        out_shape=jax.ShapeDtypeStruct((grid_size, 2, child_rows, rows_here), BF16),
        compiler_params=pltpu.CompilerParams(vmem_limit_bytes=VMEM_LIMIT),
        cost_estimate=pl.CostEstimate(
            flops=4 * child_rows * window * source_cols.shape[1],
            bytes_accessed=8 * child_rows * source_cols.shape[1],
            transcendentals=0,
        ),
    )(lane_start, source_cols, own, far)


def panels_kernel(inverse, c0, c1, c2, place, factors, solves, crosses, out_ref, parts, *, child_rows):
    tile = pl.program_id(0)
    per_device = child_rows // BLK
    units = TILE // BLK
    blocks = inverse.shape[0] // 2

    @pl.when(tile == 0)
    def _():
        for step in range(PANELS):
            for index, part in enumerate(split3(solves[step])):
                parts[step, index] = part

    rows = []
    for child in range(2):
        picked = []
        for chunk, pitch in ((c0, child_rows + EXTRA), (c1, child_rows), (c2, child_rows)):
            pieces = []
            for unit in range(units):
                block = inverse[child * blocks + tile * units + unit]
                safe = jnp.maximum(block, 0)
                at = (safe // per_device) * pitch + (safe % per_device) * BLK
                at = pl.multiple_of(at, 16)
                piece = chunk[pl.ds(at, BLK), child * PW : (child + 1) * PW].astype(F32)
                pieces.append(jnp.where(block >= 0, piece, 0.0).astype(BF16))
            picked.append(jnp.concatenate(pieces, axis=0))
        rows.append(picked)
    done = []
    for step in range(PANELS):
        low, high = step * PW, (step + 1) * PW
        total = jnp.zeros((TILE, PW), F32)
        for child in range(2):
            for chunk in range(step + 1):
                total += jnp.dot(
                    rows[child][chunk],
                    place[child, chunk * PW : (chunk + 1) * PW, low:high],
                    preferred_element_type=F32,
                )
        current = total.astype(BF16)
        for earlier in range(step):
            cross = crosses[low:high, earlier * PW : (earlier + 1) * PW]
            current = (current.astype(F32) - dot_nt(done[earlier], cross)).astype(BF16)
        solved = dot_nt(current, parts[step, 2]) + dot_nt(current, parts[step, 1])
        solved = solved + dot_nt(current, parts[step, 0])
        parts_of = []
        for part in range(TILE // PW):
            place_of = tile * (TILE // PW) + part
            value = solved[part * PW : (part + 1) * PW]
            value = jnp.where(place_of == step, factors[step], value)
            parts_of.append(jnp.where(place_of < step, 0.0, value).astype(BF16))
        chosen = jnp.concatenate(parts_of, axis=0)
        done.append(chosen)
        out_ref[:, low:high] = chosen


def panels(inverse, chunks, place, factors, solves, crosses, front_order, child_rows):
    whole = lambda shape: pl.BlockSpec(shape, lambda t, s: (0,) * len(shape))
    return pl.pallas_call(
        functools.partial(panels_kernel, child_rows=child_rows),
        grid_spec=pltpu.PrefetchScalarGridSpec(
            num_scalar_prefetch=1,
            grid=(front_order // TILE,),
            in_specs=[whole(x.shape) for x in (*chunks, place, factors, solves, crosses)],
            out_specs=pl.BlockSpec((TILE, TOP), lambda t, s: (t, 0)),
            scratch_shapes=[pltpu.VMEM((PANELS, 3, PW, PW), BF16)],
        ),
        out_shape=jax.ShapeDtypeStruct((front_order, TOP), BF16),
        compiler_params=pltpu.CompilerParams(vmem_limit_bytes=VMEM_LIMIT),
    )(inverse, *chunks, place, factors, solves, crosses)


def trailing_kernel(scalars, src_ref, diag_ref, rows_ref, mine_ref, tile_ref, out_ref, *, child_rows):
    tile = pl.program_id(0)
    rows_here = out_ref.shape[0]
    tiles = pl.num_programs(0)
    active, first_row = scalars[2 * tiles], scalars[2 * tiles + 1]

    @pl.when(tile < PANELS)
    def _():
        for step in range(PANELS):
            @pl.when(tile == step)
            def _():
                out_ref[...] = mine_ref[:, step * PW : (step + 1) * PW]

    @pl.when(tile >= PANELS)
    def _():
        ids = lax.broadcasted_iota(jnp.int32, (PW, PW), 0)
        total = None
        per_device = child_rows // BLK
        for child in range(2):
            first = scalars[child * tiles + tile]
            pick = (ids == src_ref[child : child + 1, :] - first * BLK).astype(F32).astype(BF16)
            pieces = []
            for unit in range(UNIT):
                block = first + unit
                at = ((block // per_device) * 2 + child) * child_rows + (block % per_device) * BLK
                pieces.append(rows_ref[pl.ds(pl.multiple_of(at, BLK), BLK), :])
            term = lax.dot_general(
                jnp.concatenate(pieces, axis=0), pick, (((0,), (0,)), ((), ())),
                preferred_element_type=F32,
            )
            total = term if total is None else total + term
        row = first_row + lax.broadcasted_iota(jnp.int32, (rows_here, PW), 0)
        col = tile * PW + lax.broadcasted_iota(jnp.int32, (rows_here, PW), 1)
        on_diag = row == col
        total = total + jnp.where(on_diag, diag_ref[...], 0.0)
        padding = (row >= active) | (col >= active)
        current = jnp.where(padding, jnp.where(on_diag, 1.0, 0.0), total).astype(BF16)
        for step in range(PANELS):
            low, high = step * PW, (step + 1) * PW
            product = dot_nt(mine_ref[:, low:high], tile_ref[:, low:high])
            current = (current.astype(F32) - product).astype(BF16)
        out_ref[...] = jnp.where(row < TOP, 0.0, current.astype(F32)).astype(BF16)


def trailing(scalars, source_rows, diag, rows, mine, factor, child_rows):
    front_order = factor.shape[0]
    rows_here = mine.shape[0]
    tiles = front_order // PW
    whole = lambda x: pl.BlockSpec(x.shape, lambda t, s: (0,) * x.ndim)
    return pl.pallas_call(
        functools.partial(trailing_kernel, child_rows=child_rows),
        grid_spec=pltpu.PrefetchScalarGridSpec(
            num_scalar_prefetch=1,
            grid=(tiles,),
            in_specs=[
                pl.BlockSpec((2, PW), lambda t, s: (0, t)),
                whole(diag), whole(rows), whole(mine),
                pl.BlockSpec((PW, TOP), lambda t, s: (t, 0)),
            ],
            out_specs=pl.BlockSpec((rows_here, PW), lambda t, s: (0, t)),
        ),
        out_shape=jax.ShapeDtypeStruct((rows_here, front_order), BF16),
        compiler_params=pltpu.CompilerParams(vmem_limit_bytes=VMEM_LIMIT),
    )(scalars, source_rows, diag, rows, mine, factor)


def pivot_chain(tops):
    factors, inverses, rows_of = [], [], []
    for step in range(PANELS):
        low = step * PW
        current = tops[step][low:]
        for earlier in range(step):
            lower = rows_of[earlier][low:]
            product = dot_nt(lower, lower[:PW])
            current = rounded(current - product)
        factor, inverse = pivot_parts(current[:PW])
        factors.append(factor)
        inverses.append(inverse)
        below = rounded(highest(current[PW:], inverse.T)).astype(BF16)
        head = jnp.zeros((low + PW, PW), BF16)
        rows_of.append(jnp.concatenate([head, below], axis=0))
    return jnp.stack(factors), jnp.stack(inverses), jnp.concatenate(rows_of, axis=1)


def body(front_diag, children, parent, front_blocks, child_blocks, row_map):
    leaf_id = lax.axis_index("leaf")
    grid_id = lax.axis_index("grid")
    grid_size = lax.axis_size("grid")
    rows_here = front_diag.shape[1]
    front_order = rows_here * grid_size
    child_rows = children.shape[1]
    child_order = children.shape[2]
    blocks_front = front_order // BLK
    blocks_child = child_order // BLK
    partner = jnp.bitwise_xor(leaf_id, 1)
    first_child = 2 * leaf_id
    keep_first = parent[first_child] == leaf_id
    own_child = jnp.where(keep_first, first_child, first_child + 1)
    partner_first = 2 * partner
    far_child = jnp.where(parent[partner_first] == leaf_id, partner_first, partner_first + 1)
    own_part = jnp.where(keep_first, children[0], children[1])
    away_part = jnp.where(keep_first, children[1], children[0])

    strip_far = swapped(away_part[:, :TOP], "leaf", 0)
    arrived = swapped(away_part, "leaf", 0)
    high_part = rounded(front_diag[0])
    mid_part = rounded(front_diag[0] - high_part)
    low_part = front_diag[0] - high_part - mid_part
    packed = jnp.concatenate([high_part, mid_part, low_part]).astype(BF16)
    packed = jnp.pad(packed, (0, EXTRA * 2 * PW - 3 * rows_here)).reshape(EXTRA, 2 * PW)
    chunks = []
    for step in range(PANELS):
        low, high = step * PW, (step + 1) * PW
        pair = jnp.concatenate([own_part[:, low:high], strip_far[:, low:high]], axis=1)
        if step == 0:
            pair = jnp.concatenate([pair, packed], axis=0)
        chunks.append(lax.all_gather(pair, "grid", axis=0, tiled=True))

    ids = jnp.stack([own_child, far_child])
    maps = row_map[ids]
    live = jnp.arange(blocks_child)[None, :] < child_blocks[ids][:, None]
    hits = (maps[:, :, None] == jnp.arange(blocks_front)[None, None, :]) & live[:, :, None]
    inverse = jnp.max(jnp.where(hits, jnp.arange(blocks_child)[None, :, None], -1), axis=1)
    source = jnp.where(
        inverse[:, :, None] >= 0, inverse[:, :, None] * BLK + jnp.arange(BLK), -(2**20)
    ).reshape(2, front_order).astype(jnp.int32)
    filled = (inverse >= 0).astype(jnp.int32)
    before = jnp.cumsum(filled, axis=1) - filled
    per_device = rows_here // BLK
    window = (per_device + 2) * BLK
    lane_start = jnp.minimum(before[:, ::per_device] // 2, (child_order - window) // 128)
    row_start = jnp.minimum(before[:, ::UNIT], blocks_child - UNIT)

    outgoing = spread(own_part, arrived, lane_start.reshape(-1), source, grid_size, window)
    incoming = lax.all_to_all(outgoing, "grid", split_axis=0, concat_axis=0, tiled=True)

    devices = -(-TOP // child_rows)
    first_chunk = chunks[0][: devices * (child_rows + EXTRA)]
    first_chunk = first_chunk.reshape(devices, child_rows + EXTRA, 2 * PW)[:, :child_rows]
    heads = [first_chunk.reshape(devices * child_rows, 2 * PW)[:TOP]]
    heads += [chunk[:TOP] for chunk in chunks[1:]]
    holders = -(-TOP // rows_here)
    carried = chunks[0][: holders * (child_rows + EXTRA)]
    carried = carried.reshape(holders, child_rows + EXTRA, 2 * PW)[:, child_rows:]
    carried = carried.reshape(holders, -1)[:, : 3 * rows_here].reshape(holders, 3, rows_here)
    carried = carried.astype(F32)
    diag_top = ((carried[:, 2] + carried[:, 1]) + carried[:, 0]).reshape(-1)[:TOP]

    place = (jnp.arange(TOP)[None, :, None] == source[:, None, :TOP]).astype(BF16)
    tops = []
    for step in range(PANELS):
        low, high = step * PW, (step + 1) * PW
        total = jnp.zeros((TOP, PW), F32)
        for child in range(2):
            part = jnp.zeros((TOP, PW), F32)
            for chunk in range(step + 1):
                rows = heads[chunk][:, child * PW : (child + 1) * PW]
                part = part + jnp.dot(
                    rows, place[child, chunk * PW : (chunk + 1) * PW, low:high],
                    preferred_element_type=F32,
                )
            total = total + lax.dot_general(
                place[child], part.astype(BF16), (((0,), (0,)), ((), ())),
                preferred_element_type=F32,
            )
        shifted = jnp.arange(TOP)[:, None] == jnp.arange(low, high)[None, :]
        total = total + jnp.where(shifted, diag_top[:, None], 0.0)
        tops.append(rounded(total))
    factors, inverses, crosses = pivot_chain(tops)
    factor = panels(
        inverse.reshape(-1).astype(jnp.int32), chunks, place, factors, inverses, crosses, front_order, child_rows
    )
    mine = lax.dynamic_slice_in_dim(factor, grid_id * rows_here, rows_here, axis=0)
    scalars = jnp.concatenate(
        [row_start.reshape(-1), (front_blocks[leaf_id] * BLK)[None], (grid_id * rows_here)[None]]
    ).astype(jnp.int32)
    matrix = trailing(
        scalars, source, front_diag[0][:, None],
        incoming.reshape(2 * child_order, rows_here), mine, factor, child_rows,
    )
    return matrix[None]


def solution(mesh):
    in_specs = (P("leaf", "grid"), P("leaf", "grid", None), P(), P(), P(), P())
    out_specs = P("leaf", "grid", None)
    return jax.shard_map(body, mesh=mesh, in_specs=in_specs, out_specs=out_specs, check_vma=False)
```

time: 538 us -> 472 us (0.88)
  waiting for transfers between devices: 8.52 us -> 148 us
  blocking collectives: 109 us -> 0 us
  starting transfers between devices: 50.4 us -> 11.5 us
  other arithmetic: 178 us -> 152 us
  Pallas kernels: 107 us -> 92.5 us
  local copies, waits for them, and re-layouts: 24 us -> 13 us
    all_gather x1 -> x0, blocking collectives: 109 us -> none  [body(): diag_all = lax.all_gather(front_diag[0], 'grid', axis=0, tiled=True)]
    all_gather x3, waiting for transfers between devices: 0.02 us -> 97.4 us  [body(): chunks.append(lax.all_gather(pair, 'grid', axis=0, tiled=True))]
    ppermute x2, waiting for transfers between devices: 8.44 us -> 50.1 us  [swapped(): return lax.ppermute(value, axis, pairs)]
    all_to_all x2 -> x1, starting transfers between devices: 45.5 us -> 6.12 us  [body(): lax.all_to_all(outgoing, 'grid', split_axis=0, concat_axis=0, tiled=True)]
    another operation x25 -> x31, other arithmetic: 164 us -> 140 us  [the longest x18 74.6 us: triangular_parts(): factor = jnp.linalg.cholesky(block, symmetrize_input=False)]
    another operation x28 -> x3, local copies, waits for them, and re-layouts: 11.9 us -> 0.26 us  [triangular_parts(): jax.scipy.linalg.solve_triangular(factor, identity, lower=True)]
    pallas_call x2 -> x1, Pallas kernels: 24.4 us -> 14.7 us  [spread(): pl.pallas_call(functools.partial(spread_kernel, window=window), grid_spec...]
    dot_general x6, matrix products: 11.2 us -> 5.38 us  [body(): jnp.dot(rows, place[child, chunk * PW:(chunk + 1) * PW, low:high], prefer...]
  transfers between devices with their start and end apart: 7 -> 6, of which waited for: 1 -> 4; matrix products, arithmetic and copies ran while one was open for 44% -> 41% of each run, Pallas kernels for 14% -> 13%
where the time goes in v2:
time: 472 us; the launch traced here: 463 us
  other arithmetic  152 us (32%)
  waiting for transfers between devices  148 us (31%)
  Pallas kernels  92.5 us (20%)
  matrix products  31 us (7%)
  between operations  15.9 us (3%)
  local copies, waits for them, and re-layouts  13 us (3%)
  starting transfers between devices  11.5 us (2%)
    all_gather x3, waiting for transfers between devices, body(): chunks.append(lax.all_gather(pair, 'grid', axis=0, tiled=True))  97.4 us
    another operation x18, other arithmetic, triangular_parts(): factor = jnp.linalg.cholesky(block, symmetrize_input=False)  74.6 us
    another operation x12, other arithmetic, triangular_parts(): jax.scipy.linalg.solve_triangular(factor, identity, lower=True)  65.5 us
    ppermute x2, waiting for transfers between devices, swapped(): return lax.ppermute(value, axis, pairs)  50.1 us
    pallas_call x1, Pallas kernels, panels(): pl.pallas_call(functools.partial(panels_kernel, child_rows=child_rows), g...  45.8 us
    pallas_call x1, Pallas kernels, trailing(): pl.pallas_call(functools.partial(trailing_kernel, child_rows=child_rows),...  32 us
    dot_general x6, matrix products, body(): lax.dot_general(place[child], part.astype(BF16), (((0,), (0,)), ((), ()))...  16.6 us
    pallas_call x1, Pallas kernels, spread(): pl.pallas_call(functools.partial(spread_kernel, window=window), grid_spec...  14.7 us
  transfers between devices with their start and end apart: 6, of which 4 were waited for; matrix products, arithmetic and copies ran while one was open for 41% of the time, Pallas kernels for 13%

profile of v2, /device:TPU:0, one launch (start us, length us, event | category | flops | bytes accessed | tf_op | source)
XLA Modules:
  0.0 463.3 jit_solution(6183646317330036124)
XLA Ops:
  6.5 1.3 fusion.106
  8.5 2.5 select_bitcast_fusion
  11.1 1.3 copy-done.4
  12.4 3.0 collective-permute-start.1
  15.5 9.0 %collective-permute-done.1 = bf16[256,768]{1,0:T(8,128)(2,1)S(1)} collective-permute-done((bf16[256,768]{1,0:T(8,128)(2,1)S(1)}, bf16[256,768]{1,0:T(8,128)(2,1)S(1)}, u32[]{:S(2)}, u32[]{:S(2)}) %collective-permute-start.1) | collective-permute-done | bytes 393248 | tf_op jit(solution)/shard_map/ppermute | solution.py:24
  24.5 0.7 fusion.105
  25.2 0.7 pad_maximum_fusion.2
  26.0 0.7 pad_maximum_fusion.3
  26.7 1.8 collective-permute-start
  29.7 0.6 gather_fusion.1
  32.2 0.7 add_select_fusion.src_ref
  32.9 41.0 %collective-permute-done.far_ref = bf16[256,4096]{1,0:T(8,128)(2,1)} collective-permute-done((bf16[256,4096]{1,0:T(8,128)(2,1)}, bf16[256,4096]{1,0:T(8,128)(2,1)}, u32[]{:S(2)}, u32[]{:S(2)}) %collective-permute-start) | collective-permute-done | bytes 2097184 | tf_op jit(solution)/shard_map/ppermute | solution.py:24
  73.9 14.7 %shard_map.64 = bf16[16,2,256,512]{3,2,1,0:T(8,128)(2,1)} custom-call(s32[32]{0:T(128)} %reshape.181.lane_start, s32[2,8192]{1,0:T(2,128)} %add_select_fusion.src_ref, bf16[256,4096]{1,0:T(8,128)(2,1)} %copy-done.3, bf16[256,4096]{1,0:T(8,128)(2,1)} %collective-permute-done.far_ref), custom_call_target="tpu_custom_call" | custom-call | flops 5368709120 | bytes 16777216 | tf_op jit(solution)/shard_map/pallas_call | solution.py:77
  88.6 6.1 %all-to-all-start = ((bf16[16,2,256,512]{3,2,1,0:T(8,128)(2,1)}), bf16[16,2,256,512]{3,2,1,0:T(8,128)(2,1)}, u32[]{:S(2)}, u32[]{:S(2)}) async-start(bf16[16,2,256,512]{3,2,1,0:T(8,128)(2,1)} %shard_map.64), calls=%async_computation | async-start | bytes 16777216 | tf_op jit(solution)/shard_map/all_to_all | solution.py:303
  95.6 0.9 copy.41.diag_ref
  96.4 0.7 dynamic_slice.14
  97.7 0.6 pad_add_fusion.scalars
  98.3 2.6 iota_compare_fusion
  100.9 0.7 pad_maximum_fusion.4
  101.7 1.1 slice-done
  103.1 1.7 fusion.11
  104.9 2.2 fusion.4
  107.1 11.7 %cholesky.105 = f32[128,128]{1,0:T(8,128)S(1)} custom-call(f32[128,128]{1,0:T(8,128)S(1)} %slice.284), custom_call_target="Cholesky" | custom-call | tf_op jit(solution)/shard_map/jit(cholesky)/cholesky | solution.py:36
  119.4 1.2 select_bitcast_fusion.7
  120.6 9.8 %custom-call.10 = f32[1,128,128]{1,2,0:T(8,128)S(1)} custom-call(f32[1,128,128]{2,1,0:T(8,128)S(1)} %get-tuple-element.17), custom_call_target="InvertDiagBlocksLowerTriangular" | custom-call | tf_op jit(solution)/shard_map/jit(_solve_triangular)/triangular_solve | solution.py:38
  131.0 0.7 copy.30
  132.0 11.9 %cholesky.116 = f32[128,128]{1,0:T(8,128)S(1)} custom-call(f32[128,128]{1,0:T(8,128)S(1)} %convolution_subtract_fusion.5), custom_call_target="Cholesky" | custom-call | tf_op jit(solution)/shard_map/jit(cholesky)/cholesky | solution.py:36
  143.9 0.7 compare_reduce_fusion.4
  144.7 1.3 select_bitcast_fusion.6
  146.0 9.8 %custom-call.11 = f32[1,128,128]{1,2,0:T(8,128)S(1)} custom-call(f32[1,128,128]{2,1,0:T(8,128)S(1)} %get-tuple-element.15), custom_call_target="InvertDiagBlocksLowerTriangular" | custom-call | tf_op jit(solution)/shard_map/jit(_solve_triangular)/triangular_solve | solution.py:38
  156.8 0.6 fusion.15
  157.4 1.2 fusion.42
  158.8 74.6 %all-gather.6.cloned.1.call-done.c1 = bf16[4096,512]{1,0:T(8,128)(2,1)} async-done(((bf16[256,512]{1,0:T(8,128)(2,1)}), bf16[4096,512]{1,0:T(8,128)(2,1)}) %all-gather.6.cloned.1.call-update) | async-done | bytes 4194320 | tf_op jit(solution)/shard_map/all_gather | solution.py:285
  233.5 3.2 fusion.10
  236.7 2.9 fusion.13
  239.6 1.5 fusion.14
  241.1 11.7 %cholesky.127 = f32[128,128]{1,0:T(8,128)S(1)} custom-call(f32[128,128]{1,0:T(8,128)S(1)} %slice.298), custom_call_target="Cholesky" | custom-call | tf_op jit(solution)/shard_map/jit(cholesky)/cholesky | solution.py:36
  252.8 0.7 compare_reduce_fusion.3
  253.5 1.3 select_bitcast_fusion.5
  254.8 10.0 %custom-call.12 = f32[1,128,128]{1,2,0:T(8,128)S(1)} custom-call(f32[1,128,128]{2,1,0:T(8,128)S(1)} %get-tuple-element.13), custom_call_target="InvertDiagBlocksLowerTriangular" | custom-call | tf_op jit(solution)/shard_map/jit(_solve_triangular)/triangular_solve | solution.py:38
  265.3 0.7 copy.34
  266.3 11.7 %cholesky.138 = f32[128,128]{1,0:T(8,128)S(1)} custom-call(f32[128,128]{1,0:T(8,128)S(1)} %convolution_subtract_fusion.4), custom_call_target="Cholesky" | custom-call | tf_op jit(solution)/shard_map/jit(cholesky)/cholesky | solution.py:36
  278.1 0.6 compare_reduce_fusion.2
  278.7 1.3 select_bitcast_fusion.4
  280.0 9.8 %custom-call.13 = f32[1,128,128]{1,2,0:T(8,128)S(1)} custom-call(f32[1,128,128]{2,1,0:T(8,128)S(1)} %get-tuple-element.11), custom_call_target="InvertDiagBlocksLowerTriangular" | custom-call | tf_op jit(solution)/shard_map/jit(_solve_triangular)/triangular_solve | solution.py:38
  292.0 2.1 convolution_add_fusion.4
  294.1 1.3 convolution_add_fusion.2
  295.4 22.8 %all-gather.8.cloned.1.call-done.c2 = bf16[4096,512]{1,0:T(8,128)(2,1)} async-done(((bf16[256,512]{1,0:T(8,128)(2,1)}), bf16[4096,512]{1,0:T(8,128)(2,1)}) %all-gather.8.cloned.1.call-update) | async-done | bytes 4194320 | tf_op jit(solution)/shard_map/all_gather | solution.py:285
  318.2 3.2 fusion.9
  321.4 3.3 fusion.12
  324.7 1.3 fusion.19
  326.3 11.7 %cholesky.149 = f32[128,128]{1,0:T(8,128)S(1)} custom-call(f32[128,128]{1,0:T(8,128)S(1)} %slice.314), custom_call_target="Cholesky" | custom-call | tf_op jit(solution)/shard_map/jit(cholesky)/cholesky | solution.py:36
  338.0 0.7 compare_reduce_fusion.1
  338.7 0.6 select_bitcast_fusion.3
  339.3 9.8 %custom-call.14 = f32[1,128,128]{1,2,0:T(8,128)S(1)} custom-call(f32[1,128,128]{2,1,0:T(8,128)S(1)} %get-tuple-element.9), custom_call_target="InvertDiagBlocksLowerTriangular" | custom-call | tf_op jit(solution)/shard_map/jit(_solve_triangular)/triangular_solve | solution.py:38
  350.1 11.7 %cholesky.160 = f32[128,128]{1,0:T(8,128)S(1)} custom-call(f32[128,128]{1,0:T(8,128)S(1)} %convolution_subtract_fusion.3), custom_call_target="Cholesky" | custom-call | tf_op jit(solution)/shard_map/jit(cholesky)/cholesky | solution.py:36
  361.9 0.7 compare_reduce_fusion
  362.5 0.6 select_bitcast_fusion.2
  363.2 9.9 %custom-call.15 = f32[1,128,128]{1,2,0:T(8,128)S(1)} custom-call(f32[1,128,128]{2,1,0:T(8,128)S(1)} %get-tuple-element.6), custom_call_target="InvertDiagBlocksLowerTriangular" | custom-call | tf_op jit(solution)/shard_map/jit(_solve_triangular)/triangular_solve | solution.py:38
  374.3 1.3 pad_maximum_fusion
  375.6 1.1 fusion.17.crosses
  376.7 45.8 %shard_map.65.tile_ref = bf16[8192,768]{1,0:T(8,128)(2,1)} custom-call(s32[256]{0:T(256)} %bitcast.151, bf16[4352,512]{1,0:T(8,128)(2,1)} %all-gather.4.cloned.1.call-done.c0, bf16[4096,512]{1,0:T(8,128)(2,1)} %all-gather.6.cloned.1.call-done.c1, bf16[4096,512]{1,0:T(8,128)(2,1)} %all-gather.8.cloned.1.call-done.c2, ...), custom_call_target="tpu_custom_call" | custom-call | tf_op jit(solution)/shard_map/pallas_call | solution.py:155
  422.5 2.1 constant_dynamic-slice_fusion.mine_ref
  424.6 32.0 %shard_map.66 = bf16[512,8192]{1,0:T(8,128)(2,1)} custom-call(s32[66]{0:T(128)} %pad_add_fusion.scalars, s32[2,8192]{1,0:T(2,128)} %add_select_fusion.src_ref, f32[512,1]{1,0:T(8,128)} %copy.41.diag_ref, bf16[8192,512]{1,0:T(8,128)(2,1)} %bitcast.9.rows_ref, bf16[512,768]{1,0:T(8,128)(2,1)} %constant_dynamic-slice_fusion.mine_ref, ...), custom_call_target="tpu_custom_call" | custom-call | tf_op jit(solution)/shard_map/pallas_call | solution.py:218
  (131 shorter events, 11.7 us)
Async XLA Ops:
  6.5 22.6 %copy-start = (s32[4,64]{1,0:T(4,128)S(1)}, s32[4,64]{1,0:T(4,128)}, u32[]{:S(2)}) copy-start(s32[4,64]{1,0:T(4,128)} %param.14) | copy-start | bytes 3076
  6.5 95.2 %all-gather.4.cloned.1.call-start = ((), (), s32[]{:S(2)}) async-start(), calls=%async_computation.1 | async-start | bytes 4734976 | tf_op jit(solution)/shard_map/all_gather | solution.py:285
  8.5 6.9 %copy-start.17 = (f32[1,512]{1,0:T(1,128)S(1)}, f32[1,512]{1,0:T(1,128)}, u32[]{:S(2)}) copy-start(f32[1,512]{1,0:T(1,128)} %param.9) | copy-start | bytes 6148
  11.0 1.3 copy-start.4
  11.0 19.4 %copy-start.3 = (bf16[256,4096]{1,0:T(8,128)(2,1)}, bf16[256,4096]{1,0:T(8,128)(2,1)S(1)}, u32[]{:S(2)}) copy-start(bf16[256,4096]{1,0:T(8,128)(2,1)S(1)} %get-tuple-element.22.own_ref) | copy-start | bytes 6291460
  11.0 18.7 %copy-start.2 = (s32[4]{0:T(128)S(1)}, s32[4]{0:T(128)}, u32[]{:S(2)}) copy-start(s32[4]{0:T(128)} %param.13) | copy-start | bytes 52
  12.4 12.1 %collective-permute-start.1 = (bf16[256,768]{1,0:T(8,128)(2,1)S(1)}, bf16[256,768]{1,0:T(8,128)(2,1)S(1)}, u32[]{:S(2)}, u32[]{:S(2)}) collective-permute-start(bf16[256,768]{1,0:T(8,128)(2,1)S(1)} %slice.263), channel_id=1, source_target_pairs={{0,16},{16,0},{1,17},{17,1},{2,18},{18,2},{3,19},{19,3},{4,20},{20... | collective-permute-start | bytes 1179656 | tf_op jit(solution)/shard_map/ppermute | solution.py:24
  25.9 207.5 %all-gather.6.cloned.1.call-start = ((), (), s32[]{:S(2)}) async-start(), calls=%async_computation.2 | async-start | bytes 4456448 | tf_op jit(solution)/shard_map/all_gather | solution.py:285
  26.7 47.2 %collective-permute-start = (bf16[256,4096]{1,0:T(8,128)(2,1)}, bf16[256,4096]{1,0:T(8,128)(2,1)}, u32[]{:S(2)}, u32[]{:S(2)}) collective-permute-start(bf16[256,4096]{1,0:T(8,128)(2,1)} %copy-done.4), channel_id=1, source_target_pairs={{0,16},{16,0},{1,17},{17,1},{2,18},{18,2},{3,19},{19,3},{4,20},{20... | collective-permute-start | bytes 6291464 | tf_op jit(solution)/shard_map/ppermute | solution.py:24
  30.6 58.0 %copy-start.16 = (s32[2,128]{1,0:T(2,128)}, s32[2,128]{1,0:T(2,128)S(1)}, u32[]{:S(2)}) copy-start(s32[2,128]{1,0:T(2,128)S(1)} %select_reduce_fusion.6) | copy-start | bytes 3076
  88.6 7.8 %copy-start.18 = (s32[2]{0:T(128)S(1)}, s32[2]{0:T(128)}, u32[]{:S(2)}) copy-start(s32[2]{0:T(128)} %param.12) | copy-start | bytes 28
  88.6 9.7 %slice-start.2 = ((s32[2,8192]{1,0:T(2,128)}), s32[2,768]{1,0:T(2,128)S(1)}, s32[]{:S(2)}) async-start(s32[2,8192]{1,0:T(2,128)} %add_select_fusion.src_ref), calls=%async_computation.6 | async-start | bytes 12288 | tf_op jit(solution)/shard_map/slice | solution.py:317
  88.6 335.9 %all-to-all-start = ((bf16[16,2,256,512]{3,2,1,0:T(8,128)(2,1)}), bf16[16,2,256,512]{3,2,1,0:T(8,128)(2,1)}, u32[]{:S(2)}, u32[]{:S(2)}) async-start(bf16[16,2,256,512]{3,2,1,0:T(8,128)(2,1)} %shard_map.64), calls=%async_computation | async-start | bytes 16777216 | tf_op jit(solution)/shard_map/all_to_all | solution.py:303
  94.8 6.2 %copy-start.5 = (bf16[256,256]{1,0:T(8,128)(2,1)S(1)}, bf16[256,256]{1,0:T(8,128)(2,1)}, u32[]{:S(2)}) copy-start(bf16[256,256]{1,0:T(8,128)(2,1)} %get-tuple-element.26) | copy-start | bytes 393220
  94.8 223.4 %all-gather.8.cloned.1.call-start = ((), (), s32[]{:S(2)}) async-start(), calls=%async_computation.3 | async-start | bytes 4456448 | tf_op jit(solution)/shard_map/all_gather | solution.py:285
  101.7 1.2 slice-start
  101.7 1.3 slice-start.1
  290.2 1.0 copy-start.14
  290.8 0.6 copy-start.10
  324.7 48.8 %copy-start.11 = (f32[128,128]{1,0:T(8,128)S(1)}, f32[128,128]{1,0:T(8,128)}, u32[]{:S(2)}) copy-start(f32[128,128]{1,0:T(8,128)} %copy-done.10) | copy-start | bytes 196612
  324.7 48.8 %copy-start.15 = (f32[128,128]{1,0:T(8,128)S(1)}, f32[128,128]{1,0:T(8,128)}, u32[]{:S(2)}) copy-start(f32[128,128]{1,0:T(8,128)} %copy-done.14) | copy-start | bytes 196612
  326.0 48.2 %copy-start.6 = (f32[128,128]{1,0:T(8,128)S(1)}, f32[128,128]{1,0:T(8,128)}, u32[]{:S(2)}) copy-start(f32[128,128]{1,0:T(8,128)} %get-tuple-element.18) | copy-start | bytes 196612
  326.0 48.2 %copy-start.7 = (f32[128,128]{1,0:T(8,128)S(1)}, f32[128,128]{1,0:T(8,128)}, u32[]{:S(2)}) copy-start(f32[128,128]{1,0:T(8,128)} %get-tuple-element.16) | copy-start | bytes 196612
  326.0 48.2 %copy-start.12 = (f32[128,128]{1,0:T(8,128)S(1)}, f32[128,128]{1,0:T(8,128)}, u32[]{:S(2)}) copy-start(f32[128,128]{1,0:T(8,128)} %copy.30) | copy-start | bytes 196612
  326.3 48.0 %copy-start.8 = (f32[128,128]{1,0:T(8,128)S(1)}, f32[128,128]{1,0:T(8,128)}, u32[]{:S(2)}) copy-start(f32[128,128]{1,0:T(8,128)} %get-tuple-element.14) | copy-start | bytes 196612
  326.3 48.0 %copy-start.9 = (f32[128,128]{1,0:T(8,128)S(1)}, f32[128,128]{1,0:T(8,128)}, u32[]{:S(2)}) copy-start(f32[128,128]{1,0:T(8,128)} %get-tuple-element.12) | copy-start | bytes 196612
  326.3 48.0 %copy-start.13 = (f32[128,128]{1,0:T(8,128)S(1)}, f32[128,128]{1,0:T(8,128)}, u32[]{:S(2)}) copy-start(f32[128,128]{1,0:T(8,128)} %copy.34) | copy-start | bytes 196612
  424.5 32.0 %copy-start.1 = (s32[4,64]{1,0:T(4,128)S(1)}, s32[4,64]{1,0:T(4,128)}, u32[]{:S(2)}) copy-start(s32[4,64]{1,0:T(4,128)} %param.14) | copy-start | bytes 3076
Sparse Core Ops, SparseCore 0:
  26.1 53.5 all-gather.3
  81.8 151.6 all-gather.5
  235.6 82.5 all-gather.7
